TPU v7x, 32 devices: a whole 2x2x4 slice. The times are simulated.
32 devices in a mesh: groups: 2 (over x), dp: 16 (over z, y, core).
Axes of the slice: x: 2, y: 2, z: 4, core: 2. Of those that a mesh axis runs over, the one named last changes fastest.
Arguments:
- tokens: bfloat16 [1024, 5120], P(('groups', 'dp')), parts along dimension 0, may hold values from -6 to 6
- cotangent: bfloat16 [1024, 5120], P(('groups', 'dp')), parts along dimension 0, may hold values from -6 to 6
- w_gate: bfloat16 [5120, 24576], P(None, 'dp'), may hold values from -0.078125 to 0.078125
- w_up: bfloat16 [5120, 24576], P(None, 'dp'), may hold values from -0.078125 to 0.078125
- w_down: bfloat16 [24576, 5120], P('dp'), may hold values from -0.0390625 to 0.0390625
- model_factor: bfloat16 [5120, 128], replicated, may hold values from -0.078125 to 0.078125
- hidden_factor: bfloat16 [24576, 192], P('dp'), may hold values from -0.0390625 to 0.0390625
- lengths: int32 [32], P('groups'), parts along dimension 0, may hold values from 1 to 128, 512 in all
Outputs:
- grads: float32 [32, 12288], P(('groups', 'dp')), parts along dimension 0
There are 2 independent parts, one for each index of `groups`. A program takes and returns all parts, laid end to end along the dimension named above; an argument that names none is the same for every part. Nothing has to cross between parts.
Inputs may be any that keep to these rules, and one draw needn't show every extreme that they name: The sequences' lengths in packing order; they sum to 512.
All inputs are finite; a program needn't handle non-finite values.
Results may differ from a plain program's by a relative error of at most 0.0029.
Values may be sent and summed in bfloat16 or wider, within the bound.
A program may use at most 128 MiB of HBM per device.

v0:
```python
import jax
import jax.numpy as jnp
from jax import lax
from jax.sharding import PartitionSpec as P

LMAX = 128


def forward_part(rows, w_gate, w_up):
    gate = jnp.dot(rows, w_gate, preferred_element_type=jnp.float32)
    up = jnp.dot(rows, w_up, preferred_element_type=jnp.float32)
    return (gate, up)


def backward_part(gate, up, cot_rows, w_down, hidden_factor, rank):
    sig = jax.nn.sigmoid(gate)
    hidden = (gate * sig * up).astype(jnp.bfloat16)
    back = lax.dot_general(
        cot_rows, w_down, (((1,), (1,)), ((), ())), preferred_element_type=jnp.float32
    )
    d_up = (back * gate * sig).astype(jnp.bfloat16)
    d_gate = (back * up * sig * (1.0 + gate * (1.0 - sig))).astype(jnp.bfloat16)
    feat_gate = jnp.dot(d_gate, hidden_factor[:, 0:rank], preferred_element_type=jnp.float32)
    feat_up = jnp.dot(d_up, hidden_factor[:, rank : 2 * rank], preferred_element_type=jnp.float32)
    feat_hidden = jnp.dot(
        hidden, hidden_factor[:, 2 * rank : 3 * rank], preferred_element_type=jnp.float32
    )
    return jnp.concatenate([feat_gate, feat_up, feat_hidden], axis=1)


def outer_block(left, right):
    return jnp.dot(
        left.T, right, precision=lax.Precision.HIGHEST, preferred_element_type=jnp.float32
    )


def body(tokens, cotangent, w_gate, w_up, w_down, model_factor, hidden_factor, lengths):
    rank = model_factor.shape[1] // 2
    tok_dev = tokens.shape[0]
    devices = lax.axis_size("dp")
    total = tok_dev * devices
    seqs = lengths.shape[0]
    gate, up = forward_part(lax.all_gather(tokens, "dp", axis=0, tiled=True), w_gate, w_up)
    gate_all = gate
    up_all = up
    gate = gate_all
    up = up_all
    feats = backward_part(
        gate, up, lax.all_gather(cotangent, "dp", axis=0, tiled=True), w_down, hidden_factor, rank
    )
    feat_in = jnp.dot(tokens, model_factor[:, 0:rank], preferred_element_type=jnp.float32)
    feat_out = jnp.dot(
        cotangent, model_factor[:, rank : 2 * rank], preferred_element_type=jnp.float32
    )
    mod_feat = jnp.concatenate([feat_in, feat_out], axis=1)
    ends = jnp.cumsum(lengths)
    starts = ends - lengths
    me_index = lax.axis_index("dp")
    seq_ids = jnp.arange(seqs, dtype=jnp.int32)
    owners = jnp.arange(LMAX * lax.axis_size("dp") // LMAX, dtype=jnp.int32)
    match = owners[:, None] == seq_ids[None, :]
    first_tok = jnp.sum(jnp.where(match, starts[None, :], 0), axis=1)
    seq_len = jnp.sum(jnp.where(match, lengths[None, :], 0), axis=1)
    position = jnp.arange(LMAX, dtype=jnp.int32)
    token_at = (first_tok[:, None] + position[None, :]).reshape(LMAX * lax.axis_size("dp"))
    valid = (position[None, :] < seq_len[:, None]).reshape(LMAX * lax.axis_size("dp"))
    hid_rows = jnp.take(feats, jnp.clip(token_at, 0, total - 1), axis=0)
    hid_rows = jnp.where(valid[:, None], hid_rows, 0.0)
    local = token_at - me_index * tok_dev
    mine = valid & (local >= 0) & (local < tok_dev)
    mod_rows = jnp.take(mod_feat, jnp.clip(local, 0, tok_dev - 1), axis=0)
    mod_rows = jnp.where(mine[:, None], mod_rows, 0.0)
    slots = lax.psum_scatter(
        jnp.concatenate([hid_rows, mod_rows], axis=1), "dp", scatter_dimension=0, tiled=True
    )
    gate_feat = slots[:, 0:rank]
    up_feat = slots[:, rank : 2 * rank]
    hidden_feat = slots[:, 2 * rank : 3 * rank]
    in_feat = slots[:, 3 * rank : 4 * rank]
    out_feat = slots[:, 4 * rank : 5 * rank]
    first = outer_block(in_feat, gate_feat).reshape(1, rank * rank)
    second = outer_block(in_feat, up_feat).reshape(1, rank * rank)
    third = outer_block(hidden_feat, out_feat).reshape(1, rank * rank)
    grads = jnp.concatenate([first, second, third], axis=1)
    return grads


def solution(mesh):
    placed = (
        P(("groups", "dp"), None),
        P(("groups", "dp"), None),
        P(None, "dp"),
        P(None, "dp"),
        P("dp", None),
        P(),
        P("dp", None),
        P("groups"),
    )
    return jax.shard_map(
        body, mesh=mesh, in_specs=placed, out_specs=P(("groups", "dp"), None), check_vma=False
    )
```

profile of v0, /device:TPU:0, one launch (start us, length us, event | category | flops | bytes accessed | tf_op | source)
XLA Modules:
  0.0 226.9 jit_solution(1998606136300734024)
XLA Ops:
  6.5 0.7 all-gather.5.cloned.1.call-update
  7.3 0.7 all-gather.3.cloned.1.call-update
  8.1 0.7 copy.13
  9.6 0.8 select_reduce_fusion
  10.4 2.0 fusion.3
  12.3 1.8 fusion.5
  14.3 5.5 %gather_fusion.1 = f32[2048,128]{1,0:T(8,128)S(1)} fusion(f32[32,128]{1,0:T(8,128)S(1)} %pad_maximum_fusion.3, s32[2048]{0:T(1024)S(1)} %broadcast_clamp_fusion), kind=kCustom, calls=%fused_computation.1 | custom fusion | bytes 2105344 | tf_op jit(solution)/shard_map/jit(_take)/gather | solution.py:71
  20.0 2.4 %select_select_fusion.1 = f32[2048,128]{1,0:T(8,128)} fusion(f32[2048,128]{1,0:T(8,128)S(1)} %gather_fusion.1, pred[2048]{0:T(1024)(128)(4,1)S(1)} %get-tuple-element.6, pred[2048]{0:T(1024)(128)(4,1)S(1)} %get-tuple-element.7), kind=kLoop, calls=%fused_computation.15 | loop fusion | flops 524288 | bytes 2101248 | tf_op jit(solution)/shard_map/jit(_where)/select_n | solution.py:72
  22.4 46.0 %all-gather.5.cloned.1.call-done = bf16[512,5120]{1,0:T(8,128)(2,1)} async-done(((bf16[32,5120]{1,0:T(8,128)(2,1)}), bf16[512,5120]{1,0:T(8,128)(2,1)}) %all-gather.5.cloned.1.call-update) | async-done | bytes 5242896 | tf_op jit(solution)/shard_map/all_gather | solution.py:43
  68.4 14.1 %fusion.34 = f32[512,1536]{1,0:T(8,128)S(1)} fusion(bf16[512,5120]{1,0:T(8,128)(2,1)} %all-gather.5.cloned.1.call-done, bf16[5120,1536]{1,0:T(8,128)(2,1)} %param.10), kind=kOutput, calls=%fused_computation.59 | convolution fusion | flops 8053063680 | bytes 24117248 | tf_op jit(solution)/shard_map/dot_general | solution.py:10
  82.5 12.4 %fusion.33 = f32[512,1536]{1,0:T(8,128)S(1)} fusion(bf16[512,5120]{1,0:T(8,128)(2,1)S(1)} %copy-done.1, bf16[5120,1536]{1,0:T(8,128)(2,1)} %param.11), kind=kOutput, calls=%fused_computation.58 | convolution fusion | flops 8053063680 | bytes 24117248 | tf_op jit(solution)/shard_map/dot_general | solution.py:11
  94.9 1.7 copy-done.5
  96.7 1.0 fusion.1
  97.7 27.6 %all-gather.3.cloned.1.call-done = bf16[512,5120]{1,0:T(8,128)(2,1)} async-done(((bf16[32,5120]{1,0:T(8,128)(2,1)}), bf16[512,5120]{1,0:T(8,128)(2,1)}) %all-gather.3.cloned.1.call-update) | async-done | bytes 5242896 | tf_op jit(solution)/shard_map/all_gather | solution.py:49
  125.2 12.9 %fusion.32 = f32[512,1536]{1,0:T(8,128)S(1)} fusion(bf16[512,5120]{1,0:T(8,128)(2,1)} %all-gather.3.cloned.1.call-done, bf16[1536,5120]{1,0:T(8,128)(2,1)} %param.12), kind=kOutput, calls=%fused_computation.57 | convolution fusion | flops 8053063680 | bytes 24117248 | tf_op jit(solution)/shard_map/dot_general | solution.py:18
  138.2 1.4 fusion.2
  139.6 1.0 fusion
  140.8 6.6 %gather_fusion = f32[2048,192]{1,0:T(8,128)S(1)} fusion(f32[512,192]{1,0:T(8,128)S(1)} %copy.14, s32[2048]{0:T(1024)S(1)} %broadcast_clamp_fusion.1), kind=kCustom, calls=%fused_computation | custom fusion | bytes 3153920 | tf_op jit(solution)/shard_map/jit(_take)/gather | solution.py:67
  147.5 0.7 select_select_fusion
  148.7 2.2 pad_maximum_fusion
  151.0 64.9 %reduce-scatter.2.cloned.1.call-done = f32[128,320]{1,0:T(8,128)} async-done(((f32[2048,320]{1,0:T(8,128)}), f32[128,320]{1,0:T(8,128)}) %reduce-scatter.2.cloned.1.call-update) | async-done | bytes 163856 | tf_op jit(solution)/shard_map/reduce_scatter | solution.py:73
  215.9 1.2 fusion.15
  217.2 1.2 fusion.13
  218.5 1.1 fusion.10
  (34 shorter events, 2.9 us)
Async XLA Ops:
  6.5 61.8 %all-gather.5.cloned.1.call-start = ((), (), s32[]{:S(2)}) async-start(), calls=%async_computation.2 | async-start | bytes 5570560 | tf_op jit(solution)/shard_map/all_gather | solution.py:43
  7.3 118.0 %all-gather.3.cloned.1.call-start = ((), (), s32[]{:S(2)}) async-start(), calls=%async_computation.1 | async-start | bytes 5570560 | tf_op jit(solution)/shard_map/all_gather | solution.py:49
  8.0 207.9 %reduce-scatter.2.cloned.1.call-start = ((), (), s32[]{:S(2)}) async-start(), calls=%async_computation.3 | async-start | bytes 3342336 | tf_op jit(solution)/shard_map/reduce_scatter | solution.py:73
  68.4 14.1 %copy-start.1 = (bf16[512,5120]{1,0:T(8,128)(2,1)S(1)}, bf16[512,5120]{1,0:T(8,128)(2,1)}, u32[]{:S(2)}) copy-start(bf16[512,5120]{1,0:T(8,128)(2,1)} %all-gather.5.cloned.1.call-done) | copy-start | bytes 15728644
  82.4 12.5 %copy-start.3 = (f32[512,1536]{1,0:T(8,128)}, f32[512,1536]{1,0:T(8,128)S(1)}, u32[]{:S(2)}) copy-start(f32[512,1536]{1,0:T(8,128)S(1)} %fusion.34) | copy-start | bytes 9437188
  82.5 14.2 %copy-start.2 = (bf16[1536,192]{0,1:T(8,128)(2,1)S(1)}, bf16[1536,192]{0,1:T(8,128)(2,1)}, u32[]{:S(2)}) copy-start(bf16[1536,192]{0,1:T(8,128)(2,1)} %param.14) | copy-start | bytes 1769476
  94.9 1.7 copy-start.5
  125.2 13.0 %copy-start.4 = (f32[512,1536]{1,0:T(8,128)S(1)}, f32[512,1536]{1,0:T(8,128)}, u32[]{:S(2)}) copy-start(f32[512,1536]{1,0:T(8,128)} %copy-done.3) | copy-start | bytes 9437188
  125.2 13.0 %copy-start.6 = (f32[512,1536]{1,0:T(8,128)S(1)}, f32[512,1536]{1,0:T(8,128)}, u32[]{:S(2)}) copy-start(f32[512,1536]{1,0:T(8,128)} %copy-done.5) | copy-start | bytes 9437188
  147.5 1.2 copy-start
Sparse Core Ops, SparseCore 0:
  9.6 58.6 all-gather.4
  70.6 54.5 all-gather.2
  151.1 64.7 reduce-scatter.1
where the time goes:
time: 227 us
  waiting for transfers between devices  140 us (62%)
  matrix products  50 us (22%)
  local copies, waits for them, and re-layouts  15.5 us (7%)
  between operations  13.3 us (6%)
  other arithmetic  7.98 us (4%)
    reduce_scatter x1, waiting for transfers between devices, body(): lax.psum_scatter(jnp.concatenate([hid_rows, mod_rows], axis=1), 'dp', sca...  64.9 us
    all_gather x1, waiting for transfers between devices, body(): lax.all_gather(tokens, 'dp', axis=0, tiled=True)  46 us
    all_gather x1, waiting for transfers between devices, body(): lax.all_gather(cotangent, 'dp', axis=0, tiled=True)  27.6 us
    dot_general x1, matrix products, forward_part(): gate = jnp.dot(rows, w_gate, preferred_element_type=jnp.float32)  14.1 us
    dot_general x1, matrix products, backward_part(): lax.dot_general(cot_rows, w_down, (((1,), (1,)), ((), ())), preferred_ele...  12.9 us
    dot_general x1, matrix products, forward_part(): up = jnp.dot(rows, w_up, preferred_element_type=jnp.float32)  12.4 us
    gather x1, local copies, waits for them, and re-layouts, body(): hid_rows = jnp.take(feats, jnp.clip(token_at, 0, total - 1), axis=0)  6.64 us
    gather x1, local copies, waits for them, and re-layouts, body(): mod_rows = jnp.take(mod_feat, jnp.clip(local, 0, tok_dev - 1), axis=0)  5.47 us
  transfers between devices with their start and end apart: 3, of which 3 were waited for; matrix products, arithmetic and copies ran while one was open for 18% of the time, Pallas kernels for 0%

commit v1 on v0

v1 whole, which is shorter than its diff:
```python
import functools

import jax
import jax.numpy as jnp
from jax import lax
from jax.experimental import pallas as pl
from jax.experimental.pallas import tpu as pltpu
from jax.sharding import PartitionSpec as P

MESH = pl.DeviceIdType.MESH
PIECES = 10
WSLOTS = 3
WIRE = jnp.bfloat16


def when(cond, fn):
    pl.when(cond)(fn)


def both(a, b):
    return jnp.logical_and(a, b)


def kernel(
    Z, Y, lengths, tokens, cot, w_gate, w_up, w_down, mf_hbm, hf_hbm, out,
    buf, acc_g, acc_u, acc_b, acc_m, feats, wg, wu, wd, mf, hf,
    part, r1, s2, r2, r3, s3,
    recv_sem, send_sem, own_sem, wsem, dsem, fsem, rs_send, rs_recv, z_send, z_recv,
):
    n, C = PIECES, wg.shape[1]
    K = 2 * n
    rows_dev = tokens.shape[0]
    N = Z * Y * 2
    T = N * rows_dev
    FFD = w_gate.shape[1]
    S = lengths.shape[0]
    me = lax.axis_index("dp")
    c = lax.rem(me, 2)
    y = lax.rem(me // 2, Y)
    z = me // (2 * Y)

    def index(zz, yy, cc):
        return (zz * Y + yy) * 2 + cc

    sib = index(z, y, 1 - c)
    ynb = index(z, Y - 1 - y, c)

    def column():
        for step in range(1, Z):
            yield step, lax.rem(z + step, Z)

    def own_copy(k_static):
        src = tokens if k_static < n else cot
        col = (k_static % n) * C
        return pltpu.make_async_copy(
            src.at[:, pl.ds(col, C)], buf.at[k_static, me], own_sem.at[k_static]
        )

    for k in range(K):
        own_copy(k).start()

    def weight_copies(k, slot):
        rows = pl.ds(pl.multiple_of(k * C, C), C)
        return (
            pltpu.make_async_copy(w_gate.at[rows, :], wg.at[slot], wsem.at[slot, 0]),
            pltpu.make_async_copy(w_up.at[rows, :], wu.at[slot], wsem.at[slot, 1]),
        )

    def down_copy(k, slot):
        cols = pl.ds(pl.multiple_of(k * C, C), C)
        return pltpu.make_async_copy(w_down.at[:, cols], wd.at[slot], dsem.at[slot])

    mf_copy = pltpu.make_async_copy(mf_hbm, mf, fsem.at[0])
    hf_copy = pltpu.make_async_copy(hf_hbm, hf, fsem.at[1])
    mf_copy.start()
    for j in range(WSLOTS):
        for cp in weight_copies(j, j):
            cp.start()
    hf_copy.start()
    for j in range(WSLOTS):
        down_copy(j, j).start()

    barrier = pltpu.get_barrier_semaphore()
    partners = [sib] + ([ynb] if Y > 1 else []) + [index(zz, y, c) for _, zz in column()]
    for p in partners:
        pl.semaphore_signal(barrier, inc=1, device_id={"dp": p}, device_id_type=MESH)
    pl.semaphore_wait(barrier, len(partners))

    def block(k, o, slot, dest):
        return pltpu.make_async_remote_copy(
            src_ref=buf.at[k, o],
            dst_ref=buf.at[k, o],
            send_sem=send_sem.at[k, slot],
            recv_sem=recv_sem.at[k, o],
            device_id={"dp": dest},
            device_id_type=MESH,
        )

    def wait_block(k, o):
        block(k, o, 0, sib).wait_recv()

    def send_down(k, zz):
        return block(k, index(zz, y, c), zz, index(z - 1, y, c))

    def send_up(k, zz):
        return block(k, index(zz, y, c), zz, index(z + 1, y, c))

    def send_y(k, zz):
        return block(k, index(zz, y, c), Z + zz, ynb)

    def send_sib(k, zz, yy):
        return block(k, index(zz, yy, c), 2 * Z + zz * Y + yy, sib)

    def own_sends(k):
        yield z < Z - 1, lambda: block(k, me, 2 * Z + Z * Y, index(z + 1, y, c))
        yield z > 0, lambda: block(k, me, 2 * Z + Z * Y + 1, index(z - 1, y, c))
        if Y > 1:
            yield None, lambda: send_y(k, z)
        yield None, lambda: send_sib(k, z, y)

    def relay_sends(k, r, above):
        zz = z + r if above else z - r
        if above:
            yield z > 0, lambda: send_down(k, zz)
        else:
            yield z < Z - 1, lambda: send_up(k, zz)
        if Y > 1:
            yield None, lambda: send_y(k, zz)
        yield None, lambda: send_sib(k, zz, y)

    def run(sends, act):
        for cond, make in sends:
            if cond is None:
                act(make())
            else:
                when(cond, functools.partial(lambda m: act(m()), make))

    start = lambda cp: cp.start()
    done = lambda cp: cp.wait_send()

    def here(r, above):
        return (z + r < Z) if above else (z - r >= 0)

    def own_stage(k):
        pltpu.make_async_copy(
            tokens.at[:, pl.ds(0, C)], buf.at[k, me], own_sem.at[k]
        ).wait()
        run(own_sends(k), start)

    def relay_stage(k, r):
        for above in (True, False):
            def arrived(above=above):
                zz = z + r if above else z - r
                wait_block(k, index(zz, y, c))
                run(relay_sends(k, r, above), start)
            when(here(r, above), arrived)

    def y_stage(k, r):
        for above in (True, False) if r else (True,):
            def arrived(above=above):
                zz = z + r if above else z - r
                wait_block(k, index(zz, Y - 1 - y, c))
                send_sib(k, zz, Y - 1 - y).start()
            when(here(r, above), arrived)

    def sib_stage(k):
        for zz in range(Z):
            for yy in range(Y):
                wait_block(k, index(zz, yy, 1 - c))

    acc_g[...] = jnp.zeros_like(acc_g)
    acc_u[...] = jnp.zeros_like(acc_u)
    acc_b[...] = jnp.zeros_like(acc_b)
    acc_m[...] = jnp.zeros_like(acc_m)
    mf_copy.wait()
    hf_copy.wait()
    lane = lax.broadcasted_iota(jnp.int32, (T, 128), 1)
    TILE = 256 if FFD % 256 == 0 else FFD
    RB = T // 8

    def compute(k):
        lhs = buf[k].reshape(T, C)
        kk = lax.rem(k, n)
        slot = lax.rem(kk, WSLOTS)
        mrows = pl.ds(pl.multiple_of(kk * C, C), C)
        mod = jnp.dot(lhs, mf[mrows, :], preferred_element_type=jnp.float32)
        first = k < n
        acc_m[...] += jnp.where((lane < 64) == first, mod, 0.0)

        def forward():
            for cp in weight_copies(kk, slot):
                cp.wait()

            def tile(j, carry):
                cols = pl.ds(pl.multiple_of(j * TILE, TILE), TILE)
                acc_g[:, cols] += jnp.dot(
                    lhs, wg[slot, :, cols], preferred_element_type=jnp.float32
                )
                acc_u[:, cols] += jnp.dot(
                    lhs, wu[slot, :, cols], preferred_element_type=jnp.float32
                )
                return carry

            lax.fori_loop(0, FFD // TILE, tile, 0)

            def more():
                for cp in weight_copies(kk + WSLOTS, slot):
                    cp.start()

            when(kk + WSLOTS < n, more)

        def backward():
            down_copy(kk, slot).wait()

            def tile(j, carry):
                cols = pl.ds(pl.multiple_of(j * TILE, TILE), TILE)
                acc_b[:, cols] += lax.dot_general(
                    lhs, wd[slot, cols, :], (((1,), (1,)), ((), ())),
                    preferred_element_type=jnp.float32,
                )
                return carry

            lax.fori_loop(0, FFD // TILE, tile, 0)
            when(kk + WSLOTS < n, lambda: down_copy(kk + WSLOTS, slot).start())

            def gating():
                rows = pl.ds(pl.multiple_of(kk * RB, RB), RB)
                gate = acc_g[rows, :]
                up = acc_u[rows, :]
                sig = jax.nn.sigmoid(gate)
                gs = gate * sig
                hidden = (gs * up).astype(jnp.bfloat16)
                acc_g[rows, :] = gs
                acc_u[rows, :] = up * sig * (1.0 + gate * (1.0 - sig))
                fh = jnp.dot(hidden, hf[...], preferred_element_type=jnp.float32)
                feats[rows, 128:192] = fh[:, 128:192]

            when(kk < 8, gating)

        when(first, forward)
        when(jnp.logical_not(first), backward)

    LAG = Z + 1
    AHEAD = 1

    for k in range(AHEAD):
        own_stage(k)

    def step(t, carry):
        when(t + AHEAD < K, lambda: own_stage(t + AHEAD))
        for r in range(1, Z):
            when(both(t >= r, t - r < K), functools.partial(relay_stage, t - r, r))
        if Y > 1:
            for r in range(Z):
                when(both(t >= r + 1, t - r - 1 < K), functools.partial(y_stage, t - r - 1, r))
        def ready():
            sib_stage(t - LAG)
            compute(t - LAG)
        when(t >= LAG, ready)
        return carry

    lax.fori_loop(0, K + LAG, step, 0)

    FB = 128

    def finish(i, carry):
        rows = pl.ds(pl.multiple_of(i * FB, FB), FB)
        back = acc_b[rows, :]
        d_gate = (back * acc_u[rows, :]).astype(jnp.bfloat16)
        d_up = (back * acc_g[rows, :]).astype(jnp.bfloat16)
        fg = jnp.dot(d_gate, hf[...], preferred_element_type=jnp.float32)
        fu = jnp.dot(d_up, hf[...], preferred_element_type=jnp.float32)
        feats[rows, 0:128] = jnp.where(lane[:FB] < 64, fg[:, 0:128], fu[:, 0:128])
        return carry

    lax.fori_loop(0, T // FB, finish, 0)

    right = feats[...]
    right_hi = right.astype(jnp.bfloat16)
    right_lo = (right - right_hi.astype(jnp.float32)).astype(jnp.bfloat16)
    left = acc_m[...].T
    pos = lax.broadcasted_iota(jnp.int32, (128, T), 1)
    begin = jnp.int32(0)
    G = 4
    for s0 in range(0, S, G):
        his, los = [], []
        for s in range(s0, s0 + G):
            end = begin + lengths[s]
            picked = jnp.where(both(pos >= begin, pos < end), left, 0.0)
            hi = picked.astype(jnp.bfloat16)
            his.append(hi)
            los.append((picked - hi.astype(jnp.float32)).astype(jnp.bfloat16))
            begin = end
        hi = jnp.concatenate(his, axis=0)
        lo = jnp.concatenate(los, axis=0)
        sums = (
            jnp.dot(hi, right_hi, preferred_element_type=jnp.float32)
            + jnp.dot(hi, right_lo, preferred_element_type=jnp.float32)
            + jnp.dot(lo, right_hi, preferred_element_type=jnp.float32)
        )
        for s in range(s0, s0 + G):
            one = sums[(s - s0) * 128 : (s - s0 + 1) * 128]
            cc, yy, zz = s % 2, (s // 2) % Y, s // (2 * Y)
            part[cc, yy, zz, 0:64, :] = one[0:64, 0:128]
            part[cc, yy, zz, 64:96, :] = jnp.concatenate(
                [one[64:96, 128:192], one[96:128, 128:192]], axis=1
            )

    core_send = pltpu.make_async_remote_copy(
        src_ref=part.at[1 - c], dst_ref=r1, send_sem=rs_send.at[0], recv_sem=rs_recv.at[0],
        device_id={"dp": sib}, device_id_type=MESH,
    )
    core_send.start()
    core_send.wait_recv()
    if Y > 1:
        s2[...] = (part[c, 1 - y] + r1[1 - y]).astype(WIRE)
        y_send = pltpu.make_async_remote_copy(
            src_ref=s2, dst_ref=r2, send_sem=rs_send.at[1], recv_sem=rs_recv.at[1],
            device_id={"dp": ynb}, device_id_type=MESH,
        )
        y_send.start()
        y_send.wait_recv()

    def total(zz):
        value = part[c, y, zz] + r1[y, zz]
        if Y > 1:
            value = value + r2[zz].astype(jnp.float32)
        return value

    sends = []
    for step_z, zz in column():
        s3[step_z] = total(zz).astype(WIRE)
        cp = pltpu.make_async_remote_copy(
            src_ref=s3.at[step_z], dst_ref=r3.at[step_z], send_sem=z_send.at[step_z],
            recv_sem=z_recv.at[step_z], device_id={"dp": index(zz, y, c)}, device_id_type=MESH,
        )
        cp.start()
        sends.append(cp)
    value = total(z)
    for i, cp in enumerate(sends):
        cp.wait_recv()
        value = value + r3[i + 1].astype(jnp.float32)
    out[...] = value

    core_send.wait_send()
    if Y > 1:
        y_send.wait_send()
    for cp in sends:
        cp.wait_send()

    def drain(k, carry):
        run(own_sends(k), done)
        for r in range(1, Z):
            for above in (True, False):
                when(here(r, above), functools.partial(run, list(relay_sends(k, r, above)), done))
        if Y > 1:
            for r in range(Z):
                for above in (True, False) if r else (True,):
                    zz = z + r if above else z - r
                    when(
                        here(r, above),
                        functools.partial(lambda q: send_sib(k, q, Y - 1 - y).wait_send(), zz),
                    )
        return carry

    lax.fori_loop(0, K, drain, 0)


def body(Z, Y, tokens, cotangent, w_gate, w_up, w_down, model_factor, hidden_factor, lengths):
    rows, D = tokens.shape
    FFD = w_gate.shape[1]
    N = Z * Y * 2
    T = N * rows
    n = PIECES
    C = D // n
    K = 2 * n
    f32, bf16 = jnp.float32, jnp.bfloat16
    any_spec = pl.BlockSpec(memory_space=pl.ANY)
    dma = pltpu.SemaphoreType.DMA
    out = pl.pallas_call(
        functools.partial(kernel, Z, Y),
        out_shape=jax.ShapeDtypeStruct((96, 128), f32),
        in_specs=[pl.BlockSpec(memory_space=pltpu.SMEM)] + [any_spec] * 7,
        out_specs=pl.BlockSpec(memory_space=pltpu.VMEM),
        scratch_shapes=[
            pltpu.VMEM((K, N, rows, C), bf16),
            pltpu.VMEM((T, FFD), f32),
            pltpu.VMEM((T, FFD), f32),
            pltpu.VMEM((T, FFD), f32),
            pltpu.VMEM((T, 128), f32),
            pltpu.VMEM((T, 192), f32),
            pltpu.VMEM((WSLOTS, C, FFD), bf16),
            pltpu.VMEM((WSLOTS, C, FFD), bf16),
            pltpu.VMEM((WSLOTS, FFD, C), bf16),
            pltpu.VMEM(model_factor.shape, bf16),
            pltpu.VMEM(hidden_factor.shape, bf16),
            pltpu.VMEM((2, Y, Z, 96, 128), f32),
            pltpu.VMEM((Y, Z, 96, 128), f32),
            pltpu.VMEM((Z, 96, 128), WIRE),
            pltpu.VMEM((Z, 96, 128), WIRE),
            pltpu.VMEM((Z, 96, 128), WIRE),
            pltpu.VMEM((Z, 96, 128), WIRE),
            dma((K, N)),
            dma((K, 2 * Z + Z * Y + 2)),
            dma((K,)),
            dma((WSLOTS, 2)),
            dma((WSLOTS,)),
            dma((2,)),
            dma((2,)),
            dma((2,)),
            dma((Z,)),
            dma((Z,)),
        ],
        compiler_params=pltpu.CompilerParams(
            collective_id=0, has_side_effects=True, vmem_limit_bytes=60 * 1024 * 1024
        ),
        cost_estimate=pl.CostEstimate(
            flops=6 * T * D * FFD, bytes_accessed=6 * D * FFD, transcendentals=T * FFD
        ),
    )(lengths, tokens, cotangent, w_gate, w_up, w_down, model_factor, hidden_factor)
    first = out[0:64, 0:64].reshape(1, 4096)
    second = out[0:64, 64:128].reshape(1, 4096)
    third = jnp.concatenate([out[64:96, 0:64], out[64:96, 64:128]], axis=0).T.reshape(1, 4096)
    return jnp.concatenate([first, second, third], axis=1)


def solution(mesh):
    devices = mesh.shape["dp"]
    Y = 2 if mesh.shape["groups"] == 2 else 1
    placed = (
        P(("groups", "dp"), None),
        P(("groups", "dp"), None),
        P(None, "dp"),
        P(None, "dp"),
        P("dp", None),
        P(),
        P("dp", None),
        P("groups"),
    )
    return jax.shard_map(
        functools.partial(body, devices // (2 * Y), Y),
        mesh=mesh, in_specs=placed, out_specs=P(("groups", "dp"), None), check_vma=False,
    )
```

time: 227 us -> 121 us (0.53)
  waiting for transfers between devices: 140 us -> 0 us
  Pallas kernels: 0 us -> 116 us
  matrix products: 50 us -> 0 us
  between operations: 13.3 us -> 0.03 us
  local copies, waits for them, and re-layouts: 15.5 us -> 4.33 us
  other arithmetic: 7.98 us -> 0.67 us
    pallas_call x0 -> x1, Pallas kernels: none -> 116 us  [body(): pl.pallas_call(functools.partial(kernel, Z, Y), out_shape=jax.ShapeDtypeS...]
    all_gather x2 -> x0, waiting for transfers between devices: 73.6 us -> none  [the longest x1 46 us: body(): lax.all_gather(tokens, 'dp', axis=0, tiled=True)]
    reduce_scatter x1 -> x0, waiting for transfers between devices: 64.9 us -> none  [body(): lax.psum_scatter(jnp.concatenate([hid_rows, mod_rows], axis=1), 'dp', sca...]
    dot_general x11 -> x0, matrix products: 50 us -> none  [the longest x1 14.1 us: forward_part(): gate = jnp.dot(rows, w_gate, preferred_element_type=jnp.float32)]
    gather x2 -> x0, local copies, waits for them, and re-layouts: 12.1 us -> none  [the longest x1 6.64 us: body(): hid_rows = jnp.take(feats, jnp.clip(token_at, 0, total - 1), axis=0)]
    select_n x4 -> x0, other arithmetic: 3.14 us -> none  [the longest x1 2.4 us: body(): mod_rows = jnp.where(mine[:, None], mod_rows, 0.0)]
    concatenate x4 -> x1, other arithmetic: 3.02 us -> 0.66 us  [body(): return jnp.concatenate([first, second, third], axis=1)]
  transfers between devices with their start and end apart: 3 -> 0, of which waited for: 3 -> 0; matrix products, arithmetic and copies ran while one was open for 18% -> 0% of each run, Pallas kernels for 0% -> 0%
where the time goes in v1:
time: 121 us
  Pallas kernels  116 us (96%)
  local copies, waits for them, and re-layouts  4.33 us (4%)
    pallas_call x1, Pallas kernels, body(): pl.pallas_call(functools.partial(kernel, Z, Y), out_shape=jax.ShapeDtypeS...  116 us

profile of v1, /device:TPU:0, one launch (start us, length us, event | category | flops | bytes accessed | tf_op | source)
XLA Modules:
  0.0 120.6 jit_solution(13778165405268610697)
XLA Ops:
  0.0 2.2 %copy.10.hf_hbm = bf16[1536,192]{1,0:T(8,128)(2,1)} copy(bf16[1536,192]{0,1:T(8,128)(2,1)} %param.14) | data formatting | bytes 1179648 | tf_op args[6]
  2.2 115.6 %shard_map.82 = f32[96,128]{1,0:T(8,128)} custom-call(s32[16]{0:T(128)} %lengths.1, bf16[32,5120]{1,0:T(8,128)(2,1)} %tokens.1, bf16[32,5120]{1,0:T(8,128)(2,1)} %cot.1, bf16[5120,1536]{1,0:T(8,128)(2,1)} %w_gate.1, bf16[5120,1536]{1,0:T(8,128)(2,1)} %w_up.1, bf16[1536,5120]{1,0:T(8,128)(2,1)} %w_down.1, bf16[5120,128]{1,0:T(8,128)(2,1)} %mf_hbm.1, ...), custom_call_target="tpu_custom_call" | custom-call | flops 24159191040 | bytes 47185920 | tf_op jit(solution)/shard_map/pallas_call | solution.py:380
  117.8 0.9 fusion.1
  118.7 0.1 copy.11
  118.8 0.1 reshape.11
  118.9 0.9 fusion
  119.8 0.1 reshape.9
  119.9 0.1 reshape.10
  120.0 0.7 pad_maximum_fusion
  (1 shorter events, 0.0 us)

commit v2 on v1

--- a/solution.py
+++ b/solution.py
@@ -8,8 +8,11 @@
 from jax.sharding import PartitionSpec as P
 
 MESH = pl.DeviceIdType.MESH
-PIECES = 10
-WSLOTS = 3
+PIECES = 5
+WSLOTS = 2
+Y_EVERY = 5
+HOP = 1
+AHEAD = 1
 WIRE = jnp.bfloat16
 
 
@@ -99,6 +102,9 @@
     def wait_block(k, o):
         block(k, o, 0, sib).wait_recv()
 
+    def y_first(k):
+        return lax.rem(k, Y_EVERY) == Y_EVERY // 2
+
     def send_down(k, zz):
         return block(k, index(zz, y, c), zz, index(z - 1, y, c))
 
@@ -125,8 +131,21 @@
         else:
             yield z < Z - 1, lambda: send_up(k, zz)
         if Y > 1:
-            yield None, lambda: send_y(k, zz)
+            yield jnp.logical_not(y_first(k)), lambda: send_y(k, zz)
         yield None, lambda: send_sib(k, zz, y)
+
+    def other_sends(k, r, above):
+        zz = z + r if above else z - r
+        o = index(zz, Y - 1 - y, c)
+        up, down = index(z + 1, y, c), index(z - 1, y, c)
+        base = 2 * Z + Z * Y + 2
+        if r == 0 or not above:
+            yield both(y_first(k), z < Z - 1), lambda: block(k, o, base + zz, up)
+        if r == 0:
+            yield both(y_first(k), z > 0), lambda: block(k, o, base + Z, down)
+        elif above:
+            yield both(y_first(k), z > 0), lambda: block(k, o, base + zz, down)
+        yield None, lambda: send_sib(k, zz, Y - 1 - y)
 
     def run(sends, act):
         for cond, make in sends:
@@ -160,13 +179,16 @@
             def arrived(above=above):
                 zz = z + r if above else z - r
                 wait_block(k, index(zz, Y - 1 - y, c))
-                send_sib(k, zz, Y - 1 - y).start()
+                run(other_sends(k, r, above), start)
             when(here(r, above), arrived)
 
     def sib_stage(k):
         for zz in range(Z):
             for yy in range(Y):
                 wait_block(k, index(zz, yy, 1 - c))
+
+    for k in range(AHEAD):
+        own_stage(k)
 
     acc_g[...] = jnp.zeros_like(acc_g)
     acc_u[...] = jnp.zeros_like(acc_u)
@@ -175,8 +197,14 @@
     mf_copy.wait()
     hf_copy.wait()
     lane = lax.broadcasted_iota(jnp.int32, (T, 128), 1)
-    TILE = 256 if FFD % 256 == 0 else FFD
-    RB = T // 8
+    TILE = FFD // 2
+    GATING = 8 if n >= 8 else 4
+    RB = T // GATING
+
+    def project(rows):
+        return lax.dot_general(
+            rows, hf[...], (((1,), (1,)), ((), ())), preferred_element_type=jnp.float32
+        )
 
     def compute(k):
         lhs = buf[k].reshape(T, C)
@@ -232,30 +260,31 @@
                 hidden = (gs * up).astype(jnp.bfloat16)
                 acc_g[rows, :] = gs
                 acc_u[rows, :] = up * sig * (1.0 + gate * (1.0 - sig))
-                fh = jnp.dot(hidden, hf[...], preferred_element_type=jnp.float32)
+                fh = project(hidden)
                 feats[rows, 128:192] = fh[:, 128:192]
 
-            when(kk < 8, gating)
+            when(kk < GATING, gating)
 
         when(first, forward)
         when(jnp.logical_not(first), backward)
 
-    LAG = Z + 1
-    AHEAD = 1
-
-    for k in range(AHEAD):
-        own_stage(k)
+    LAG = HOP * (Z + 1)
 
     def step(t, carry):
-        when(t + AHEAD < K, lambda: own_stage(t + AHEAD))
         for r in range(1, Z):
-            when(both(t >= r, t - r < K), functools.partial(relay_stage, t - r, r))
+            k = t - HOP * r + HOP - 1
+            when(both(k >= 0, k < K), functools.partial(relay_stage, k, r))
         if Y > 1:
             for r in range(Z):
-                when(both(t >= r + 1, t - r - 1 < K), functools.partial(y_stage, t - r - 1, r))
+                k = t - HOP * (r + 1) + HOP - 1
+                when(both(k >= 0, k < K), functools.partial(y_stage, k, r))
+
+        when(t + AHEAD < K, lambda: own_stage(t + AHEAD))
+
         def ready():
             sib_stage(t - LAG)
             compute(t - LAG)
+
         when(t >= LAG, ready)
         return carry
 
@@ -268,8 +297,8 @@
         back = acc_b[rows, :]
         d_gate = (back * acc_u[rows, :]).astype(jnp.bfloat16)
         d_up = (back * acc_g[rows, :]).astype(jnp.bfloat16)
-        fg = jnp.dot(d_gate, hf[...], preferred_element_type=jnp.float32)
-        fu = jnp.dot(d_up, hf[...], preferred_element_type=jnp.float32)
+        fg = project(d_gate)
+        fu = project(d_up)
         feats[rows, 0:128] = jnp.where(lane[:FB] < 64, fg[:, 0:128], fu[:, 0:128])
         return carry
 
@@ -306,48 +335,6 @@
                 [one[64:96, 128:192], one[96:128, 128:192]], axis=1
             )
 
-    core_send = pltpu.make_async_remote_copy(
-        src_ref=part.at[1 - c], dst_ref=r1, send_sem=rs_send.at[0], recv_sem=rs_recv.at[0],
-        device_id={"dp": sib}, device_id_type=MESH,
-    )
-    core_send.start()
-    core_send.wait_recv()
-    if Y > 1:
-        s2[...] = (part[c, 1 - y] + r1[1 - y]).astype(WIRE)
-        y_send = pltpu.make_async_remote_copy(
-            src_ref=s2, dst_ref=r2, send_sem=rs_send.at[1], recv_sem=rs_recv.at[1],
-            device_id={"dp": ynb}, device_id_type=MESH,
-        )
-        y_send.start()
-        y_send.wait_recv()
-
-    def total(zz):
-        value = part[c, y, zz] + r1[y, zz]
-        if Y > 1:
-            value = value + r2[zz].astype(jnp.float32)
-        return value
-
-    sends = []
-    for step_z, zz in column():
-        s3[step_z] = total(zz).astype(WIRE)
-        cp = pltpu.make_async_remote_copy(
-            src_ref=s3.at[step_z], dst_ref=r3.at[step_z], send_sem=z_send.at[step_z],
-            recv_sem=z_recv.at[step_z], device_id={"dp": index(zz, y, c)}, device_id_type=MESH,
-        )
-        cp.start()
-        sends.append(cp)
-    value = total(z)
-    for i, cp in enumerate(sends):
-        cp.wait_recv()
-        value = value + r3[i + 1].astype(jnp.float32)
-    out[...] = value
-
-    core_send.wait_send()
-    if Y > 1:
-        y_send.wait_send()
-    for cp in sends:
-        cp.wait_send()
-
     def drain(k, carry):
         run(own_sends(k), done)
         for r in range(1, Z):
@@ -356,14 +343,54 @@
         if Y > 1:
             for r in range(Z):
                 for above in (True, False) if r else (True,):
-                    zz = z + r if above else z - r
-                    when(
-                        here(r, above),
-                        functools.partial(lambda q: send_sib(k, q, Y - 1 - y).wait_send(), zz),
-                    )
+                    when(here(r, above), functools.partial(run, list(other_sends(k, r, above)), done))
         return carry
 
-    lax.fori_loop(0, K, drain, 0)
+    core_send = pltpu.make_async_remote_copy(
+        src_ref=part.at[1 - c], dst_ref=r1, send_sem=rs_send.at[0], recv_sem=rs_recv.at[0],
+        device_id={"dp": sib}, device_id_type=MESH,
+    )
+    core_send.start()
+    lax.fori_loop(0, n, drain, 0)
+    core_send.wait_recv()
+    if Y > 1:
+        s2[...] = (part[c, 1 - y] + r1[1 - y]).astype(WIRE)
+        y_send = pltpu.make_async_remote_copy(
+            src_ref=s2, dst_ref=r2, send_sem=rs_send.at[1], recv_sem=rs_recv.at[1],
+            device_id={"dp": ynb}, device_id_type=MESH,
+        )
+        y_send.start()
+        lax.fori_loop(n, K, drain, 0)
+        y_send.wait_recv()
+    else:
+        lax.fori_loop(n, K, drain, 0)
+
+    def total(zz):
+        value = part[c, y, zz] + r1[y, zz]
+        if Y > 1:
+            value = value + r2[zz].astype(jnp.float32)
+        return value
+
+    sends = []
+    for step_z, zz in column():
+        s3[step_z] = total(zz).astype(WIRE)
+        cp = pltpu.make_async_remote_copy(
+            src_ref=s3.at[step_z], dst_ref=r3.at[step_z], send_sem=z_send.at[step_z],
+            recv_sem=z_recv.at[step_z], device_id={"dp": index(zz, y, c)}, device_id_type=MESH,
+        )
+        cp.start()
+        sends.append(cp)
+    value = total(z)
+    for i, cp in enumerate(sends):
+        cp.wait_recv()
+        value = value + r3[i + 1].astype(jnp.float32)
+    out[...] = value
+
+    core_send.wait_send()
+    if Y > 1:
+        y_send.wait_send()
+    for cp in sends:
+        cp.wait_send()
 
 
 def body(Z, Y, tokens, cotangent, w_gate, w_up, w_down, model_factor, hidden_factor, lengths):
@@ -393,7 +420,7 @@
             pltpu.VMEM((WSLOTS, C, FFD), bf16),
             pltpu.VMEM((WSLOTS, FFD, C), bf16),
             pltpu.VMEM(model_factor.shape, bf16),
-            pltpu.VMEM(hidden_factor.shape, bf16),
+            pltpu.VMEM(hidden_factor.shape[::-1], bf16),
             pltpu.VMEM((2, Y, Z, 96, 128), f32),
             pltpu.VMEM((Y, Z, 96, 128), f32),
             pltpu.VMEM((Z, 96, 128), WIRE),
@@ -401,7 +428,7 @@
             pltpu.VMEM((Z, 96, 128), WIRE),
             pltpu.VMEM((Z, 96, 128), WIRE),
             dma((K, N)),
-            dma((K, 2 * Z + Z * Y + 2)),
+            dma((K, 3 * Z + Z * Y + 3)),
             dma((K,)),
             dma((WSLOTS, 2)),
             dma((WSLOTS,)),
@@ -417,7 +444,7 @@
         cost_estimate=pl.CostEstimate(
             flops=6 * T * D * FFD, bytes_accessed=6 * D * FFD, transcendentals=T * FFD
         ),
-    )(lengths, tokens, cotangent, w_gate, w_up, w_down, model_factor, hidden_factor)
+    )(lengths, tokens, cotangent, w_gate, w_up, w_down, model_factor, hidden_factor.T)
     first = out[0:64, 0:64].reshape(1, 4096)
     second = out[0:64, 64:128].reshape(1, 4096)
     third = jnp.concatenate([out[64:96, 0:64], out[64:96, 64:128]], axis=0).T.reshape(1, 4096)

time: 121 us -> 93 us (0.77)
  Pallas kernels: 116 us -> 89.9 us
  local copies, waits for them, and re-layouts: 4.33 us -> 2.12 us
    pallas_call x1, Pallas kernels: 116 us -> 89.9 us  [body(): pl.pallas_call(functools.partial(kernel, Z, Y), out_shape=jax.ShapeDtypeS...]
    unnamed x1 -> x0, local copies, waits for them, and re-layouts: 2.22 us -> none
where the time goes in v2:
time: 93 us; the launch traced here: 92.7 us
  Pallas kernels  89.9 us (97%)
  local copies, waits for them, and re-layouts  2.12 us (2%)
    pallas_call x1, Pallas kernels, body(): pl.pallas_call(functools.partial(kernel, Z, Y), out_shape=jax.ShapeDtypeS...  89.9 us

profile of v2, /device:TPU:0, one launch (start us, length us, event | category | flops | bytes accessed | tf_op | source)
XLA Modules:
  0.0 92.7 jit_solution(7170987091176954610)
XLA Ops:
  0.0 89.9 %shard_map.82 = f32[96,128]{1,0:T(8,128)} custom-call(s32[16]{0:T(128)} %lengths.1, bf16[32,5120]{1,0:T(8,128)(2,1)} %tokens.1, bf16[32,5120]{1,0:T(8,128)(2,1)} %cot.1, bf16[5120,1536]{1,0:T(8,128)(2,1)} %w_gate.1, bf16[5120,1536]{1,0:T(8,128)(2,1)} %w_up.1, bf16[1536,5120]{1,0:T(8,128)(2,1)} %w_down.1, bf16[5120,128]{1,0:T(8,128)(2,1)} %mf_hbm.1, ...), custom_call_target="tpu_custom_call" | custom-call | flops 24159191040 | bytes 47185920 | tf_op jit(solution)/shard_map/pallas_call | solution.py:407
  89.9 0.9 fusion.1
  90.7 0.1 copy.9
  90.8 0.1 reshape.11
  90.9 0.9 fusion
  91.8 0.1 reshape.9
  91.9 0.1 reshape.10
  92.0 0.7 pad_maximum_fusion
  (1 shorter events, 0.0 us)

commit v3 on v2

--- a/solution.py
+++ b/solution.py
@@ -197,7 +197,7 @@
     mf_copy.wait()
     hf_copy.wait()
     lane = lax.broadcasted_iota(jnp.int32, (T, 128), 1)
-    TILE = FFD // 2
+    TILE = FFD
     GATING = 8 if n >= 8 else 4
     RB = T // GATING
 

time: 93 us -> 91.6 us (0.985)
  Pallas kernels: 89.9 us -> 88.4 us
    pallas_call x1, Pallas kernels: 89.9 us -> 88.4 us  [body(): pl.pallas_call(functools.partial(kernel, Z, Y), out_shape=jax.ShapeDtypeS...]
where the time goes in v3:
time: 91.6 us; the launch traced here: 91.2 us
  Pallas kernels  88.4 us (97%)
  local copies, waits for them, and re-layouts  2.12 us (2%)
    pallas_call x1, Pallas kernels, body(): pl.pallas_call(functools.partial(kernel, Z, Y), out_shape=jax.ShapeDtypeS...  88.4 us

profile of v3, /device:TPU:0, one launch (start us, length us, event | category | flops | bytes accessed | tf_op | source)
XLA Modules:
  0.0 91.2 jit_solution(15976190308358081857)
XLA Ops:
  0.0 88.4 %shard_map.82 = f32[96,128]{1,0:T(8,128)} custom-call(s32[16]{0:T(128)} %lengths.1, bf16[32,5120]{1,0:T(8,128)(2,1)} %tokens.1, bf16[32,5120]{1,0:T(8,128)(2,1)} %cot.1, bf16[5120,1536]{1,0:T(8,128)(2,1)} %w_gate.1, bf16[5120,1536]{1,0:T(8,128)(2,1)} %w_up.1, bf16[1536,5120]{1,0:T(8,128)(2,1)} %w_down.1, bf16[5120,128]{1,0:T(8,128)(2,1)} %mf_hbm.1, ...), custom_call_target="tpu_custom_call" | custom-call | flops 24159191040 | bytes 47185920 | tf_op jit(solution)/shard_map/pallas_call | solution.py:407
  88.4 0.9 fusion.1
  89.3 0.1 copy.9
  89.3 0.1 reshape.11
  89.5 0.9 fusion
  90.4 0.1 reshape.9
  90.5 0.1 reshape.10
  90.5 0.7 pad_maximum_fusion
  (1 shorter events, 0.0 us)
